TPU v7x, 128 devices: a whole 4x4x4 slice. The times are simulated.
128 devices in a mesh: left: 8 (over y, x_hi), right: 16 (over x_lo, z, core).
Axes of the slice: x: 4 (x_hi: 2, x_lo: 2; x = x_hi * 2 + x_lo), y: 4, z: 4, core: 2. Of those that a mesh axis runs over, the one named last changes fastest.
Arguments:
- state: float32 [128, 1024, 1024], P(('left', 'right')), may hold values from -20 to 20
- left_env: bfloat16 [2, 128, 1024, 1024], P(None, ('left', 'right')), may hold values from -0.5 to 2.5
- right_env: bfloat16 [2, 128, 1024, 1024], P(None, ('left', 'right')), may hold values from -0.5 to 2.5
- site_ops: float32 [2, 4, 4], replicated, may hold values from -3 to 3
- left_live: int32 [32], replicated, may hold values from 1 to 4
- right_live: int32 [34], replicated, may hold values from 1 to 4
Outputs:
- next_vector: float32 [128, 1024, 1024], P(('left', 'right'))
- coefficients: float32 [2], replicated
All inputs are finite; a program needn't handle non-finite values.
Results may differ from a plain program's by a relative error of at most 0.0047.
Values may be sent and summed in bfloat16 or wider, within the bound.
A program may use at most 64 MiB of HBM per device.

v0:
```python
import jax
import jax.numpy as jnp
from jax import lax
from jax.sharding import PartitionSpec as P

BLOCK = 256


def from_behind(block, axis, distance):
    devices = range(lax.axis_size(axis))
    route = [(i - distance, i) for i in devices if i - distance in devices]
    return lax.ppermute(block, axis, route)


def small_lookup(table, index):
    places = jnp.arange(table.shape[0], dtype=jnp.int32)
    return jnp.sum(jnp.where(places == index, table, jnp.zeros_like(table)))


def table_entry(table, row, column):
    rows = jnp.arange(table.shape[0], dtype=jnp.int32)[:, None]
    columns = jnp.arange(table.shape[1], dtype=jnp.int32)[None, :]
    return jnp.sum(jnp.where((rows == row) & (columns == column), table, jnp.zeros_like(table)))


def per_device(state, left_env, right_env, site_ops, left_live, right_live):
    pairs = site_ops.shape[1]
    sec_size = state.shape[1]
    block_size = BLOCK
    block_index = lax.axis_index("left") * lax.axis_size("right") + lax.axis_index("right")
    own_pair = block_index % pairs
    sector = block_index // pairs
    steps = (jnp.arange(pairs, dtype=jnp.int32) + 1) // 2
    own_step = small_lookup(steps, own_pair)
    positions = jnp.arange(sec_size, dtype=jnp.int32)
    row_mask = (positions < small_lookup(left_live, sector) * block_size).astype(jnp.float32)
    col_mask = (positions < small_lookup(right_live, sector + own_step) * block_size).astype(
        jnp.float32
    )
    live = row_mask[:, None] * col_mask[None, :]
    entries = float(
        state.shape[0] * sec_size * sec_size * lax.axis_size("left") * lax.axis_size("right")
    )
    masked = state[0] * live
    start_sum = lax.psum(jnp.sum(masked * masked), ("left", "right"))
    start_mean = start_sum / entries
    vector = masked / jnp.sqrt(start_mean + 1e-06)
    rounded = vector.astype(jnp.bfloat16)
    far_two = from_behind(rounded, ("left", "right"), 2)
    far_three = from_behind(rounded, ("left", "right"), 3)
    weights = []
    for offset in (2, 3):
        source_pair = (own_pair - offset) % pairs
        valid = block_index >= offset
        weights.append(
            jnp.where(
                valid, table_entry(site_ops[0], own_pair, source_pair), jnp.zeros((), jnp.float32)
            )
        )
    source = (
        weights[0] * far_two.astype(jnp.float32) + weights[1] * far_three.astype(jnp.float32)
    ).astype(jnp.bfloat16)
    part_zero = jnp.dot(source, right_env[0, 0], preferred_element_type=jnp.float32).astype(
        jnp.bfloat16
    )
    part_one = jnp.dot(rounded, right_env[1, 0], preferred_element_type=jnp.float32).astype(
        jnp.bfloat16
    )
    diag_weight = table_entry(site_ops[1], own_pair, own_pair)
    image = jnp.dot(left_env[0, 0], part_zero, preferred_element_type=jnp.float32)
    image = image + diag_weight * jnp.dot(
        left_env[1, 0], part_one, preferred_element_type=jnp.float32
    )
    image = image * live
    alpha_value = lax.psum(jnp.sum(vector * image), ("left", "right")) / entries
    residual = image - alpha_value * vector
    beta_value = jnp.sqrt(
        lax.psum(jnp.sum(residual * residual), ("left", "right")) / entries + 1e-06
    )
    next_vector = residual / beta_value
    return (next_vector[None], jnp.stack([alpha_value, beta_value]))


def solution(mesh):
    in_specs = (
        P(("left", "right"), None, None),
        P(None, ("left", "right"), None, None),
        P(None, ("left", "right"), None, None),
        P(),
        P(),
        P(),
    )
    out_specs = (P(("left", "right"), None, None), P())
    return jax.shard_map(
        per_device, mesh=mesh, in_specs=in_specs, out_specs=out_specs, check_vma=False
    )
```

profile of v0, /device:TPU:1, one launch (start us, length us, event | category | flops | bytes accessed | tf_op | source)
XLA Modules:
  0.0 362.2 jit_solution(16959823783765346721)
XLA Ops:
  0.6 0.6 select_reduce_fusion
  1.9 1.3 fusion.36
  3.2 1.3 fusion.37
  5.8 5.3 %copy.8 = f32[1,1024,1024]{1,2,0:T(8,128)} copy(f32[1,1024,1024]{2,1,0:T(8,128)} %param.6) | data formatting | bytes 8388608 | tf_op args[0]
  11.2 4.1 %multiply_reduce_fusion.2 = f32[]{:T(128)} fusion(f32[1,1024,1024]{1,2,0:T(8,128)} %copy.8, f32[1024]{0:T(1024)S(1)} %get-tuple-element.10, f32[1024]{0:T(1024)S(1)} %get-tuple-element.9), kind=kLoop, calls=%fused_computation.8 | loop fusion | flops 4194303 | bytes 4202500 | tf_op jit(solution)/shard_map/reduce_sum | solution.py:45
  15.3 0.0 copy-start
  15.3 68.7 %psum.21 = f32[]{:T(128)} all-reduce(f32[]{:T(128)} %multiply_reduce_fusion.2), channel_id=1, replica_groups=mesh['left'=8,'right'=16] {'left','right'}, use_global_device_ids=true, to_apply=%region_5.6 | all-reduce | flops 1 | bytes 8 | tf_op jit(solution)/shard_map/psum | solution.py:45
  84.7 2.7 fusion.38
  87.4 5.5 %collective-permute-start.1 = (bf16[1024,1024]{0,1:T(8,128)(2,1)S(1)}, bf16[1024,1024]{0,1:T(8,128)(2,1)}, u32[]{:S(2)}, u32[]{:S(2)}) collective-permute-start(bf16[1024,1024]{0,1:T(8,128)(2,1)S(1)} %fusion.38), channel_id=1, source_target_pairs={{0,3},{1,4},{2,5},{3,6},{4,7},{5,8},{6,9},{7,10},{8,11},{9,12},{10... | collective-permute-start | bytes 6291464 | tf_op jit(solution)/shard_map/ppermute | solution.py:12
  92.9 2.6 collective-permute-start
  95.6 0.0 copy-done
  95.6 0.8 fusion.33
  97.6 39.5 %collective-permute-done.1 = bf16[1024,1024]{0,1:T(8,128)(2,1)} collective-permute-done((bf16[1024,1024]{0,1:T(8,128)(2,1)S(1)}, bf16[1024,1024]{0,1:T(8,128)(2,1)}, u32[]{:S(2)}, u32[]{:S(2)}) %collective-permute-start.1) | collective-permute-done | bytes 2097184 | tf_op jit(solution)/shard_map/ppermute | solution.py:12
  137.1 43.1 %collective-permute-done = bf16[1024,1024]{0,1:T(8,128)(2,1)} collective-permute-done((bf16[1024,1024]{0,1:T(8,128)(2,1)S(1)}, bf16[1024,1024]{0,1:T(8,128)(2,1)}, u32[]{:S(2)}, u32[]{:S(2)}) %collective-permute-start) | collective-permute-done | bytes 2097184 | tf_op jit(solution)/shard_map/ppermute | solution.py:12
  180.2 10.0 %fusion.6 = f32[1024,1024]{1,0:T(8,128)} fusion(bf16[2,1,1024,1024]{3,2,1,0:T(8,128)(2,1)} %param.7, bf16[1024,1024]{0,1:T(8,128)(2,1)} %collective-permute-done.1, bf16[1024,1024]{0,1:T(8,128)(2,1)} %collective-permute-done, bf16[2,1,1024,1024]{3,2,1,0:T(8,128)(2,1)} %param.8, f32[]{:T(128)S(6)} %select_n.63, f32[]{:T(128)S(6)} %select_n.55), kind=kOutput, calls=%fused_computation.15 | convolution fusion | flops 4302307328 | bytes 12582920 | tf_op jit(solution)/shard_map/dot_general | solution.py:70
  190.2 14.2 %multiply_reduce_fusion.1 = (f32[]{:T(128)}, f32[1024,1024]{0,1:T(8,128)}) fusion(f32[]{:T(128)S(6)} %sqrt.6, f32[1024]{0:T(1024)S(1)} %get-tuple-element.10, f32[1024]{0:T(1024)S(1)} %get-tuple-element.9, f32[1,1024,1024]{1,2,0:T(8,128)} %copy.8, f32[1024,1024]{1,0:T(8,128)} %fusion.6, bf16[2,1,1024,1024]{3,2,1,0:T(8,128)(2,1)} %param.7, ...), kind=kOutput, calls=%fused_computation.5 | convolution fusion | flops 4308598784 | bytes 20989444 | tf_op jit(solution)/shard_map/dot_general | solution.py:71
  204.4 75.6 %psum.22 = f32[]{:T(128)} all-reduce(f32[]{:T(128)} %get-tuple-element.7), channel_id=1, replica_groups=mesh['left'=8,'right'=16] {'left','right'}, use_global_device_ids=true, to_apply=%region_9.10 | all-reduce | flops 1 | bytes 8 | tf_op jit(solution)/shard_map/psum | solution.py:75
  280.6 5.7 %multiply_reduce_fusion = f32[]{:T(128)} fusion(f32[1024,1024]{0,1:T(8,128)} %get-tuple-element.8, f32[]{:T(128)} %div.55, f32[]{:T(128)S(6)} %sqrt.6, f32[1024]{0:T(1024)S(1)} %get-tuple-element.10, f32[1024]{0:T(1024)S(1)} %get-tuple-element.9, f32[1,1024,1024]{1,2,0:T(8,128)} %copy.8), kind=kLoop, calls=%fused_computation.3 | loop fusion | flops 7340031 | bytes 8396812 | tf_op jit(solution)/shard_map/reduce_sum | solution.py:78
  286.4 62.8 %psum.23 = f32[]{:T(128)} all-reduce(f32[]{:T(128)} %multiply_reduce_fusion), channel_id=1, replica_groups=mesh['left'=8,'right'=16] {'left','right'}, use_global_device_ids=true, to_apply=%region_11.12 | all-reduce | flops 1 | bytes 8 | tf_op jit(solution)/shard_map/psum | solution.py:78
  349.9 6.4 %divide_bitcast_fusion = f32[1,1024,1024]{1,2,0:T(8,128)} fusion(f32[]{:T(128)} %sqrt.7, f32[1024,1024]{0,1:T(8,128)} %get-tuple-element.8, f32[]{:T(128)} %div.55, f32[]{:T(128)S(6)} %sqrt.6, f32[1024]{0:T(1024)S(1)} %get-tuple-element.10, f32[1024]{0:T(1024)S(1)} %get-tuple-element.9, f32[1,1024,1024]{1,2,0:T(8,128)} %copy.8), kind=kLoop, calls=%fused_computation.2 | loop fusion | flops 6291456 | bytes 12591116 | tf_op jit(solution)/shard_map/broadcast_in_dim | solution.py:81
  356.2 5.3 %copy.9 = f32[1,1024,1024]{2,1,0:T(8,128)} copy(f32[1,1024,1024]{1,2,0:T(8,128)} %divide_bitcast_fusion) | data formatting | bytes 8388608
  361.6 0.6 pad_maximum_fusion
  (3 shorter events, 0.0 us)
Async XLA Ops:
  15.3 80.3 %copy-start = (f32[2,4,4]{2,1,0:T(4,128)S(1)}, f32[2,4,4]{2,1,0:T(4,128)}, u32[]{:S(2)}) copy-start(f32[2,4,4]{2,1,0:T(4,128)} %param.9) | copy-start | bytes 388
  87.4 49.7 %collective-permute-start.1 = (bf16[1024,1024]{0,1:T(8,128)(2,1)S(1)}, bf16[1024,1024]{0,1:T(8,128)(2,1)}, u32[]{:S(2)}, u32[]{:S(2)}) collective-permute-start(bf16[1024,1024]{0,1:T(8,128)(2,1)S(1)} %fusion.38), channel_id=1, source_target_pairs={{0,3},{1,4},{2,5},{3,6},{4,7},{5,8},{6,9},{7,10},{8,11},{9,12},{10... | collective-permute-start | bytes 6291464 | tf_op jit(solution)/shard_map/ppermute | solution.py:12
  92.9 87.3 %collective-permute-start = (bf16[1024,1024]{0,1:T(8,128)(2,1)S(1)}, bf16[1024,1024]{0,1:T(8,128)(2,1)}, u32[]{:S(2)}, u32[]{:S(2)}) collective-permute-start(bf16[1024,1024]{0,1:T(8,128)(2,1)S(1)} %fusion.38), channel_id=1, source_target_pairs={{0,2},{1,3},{2,4},{3,5},{4,6},{5,7},{6,8},{7,9},{8,10},{9,11},{10,... | collective-permute-start | bytes 6291464 | tf_op jit(solution)/shard_map/ppermute | solution.py:12
where the time goes:
time: 363 us; the launch traced here: 362 us
  blocking collectives  207 us (57%)
  waiting for transfers between devices  82.6 us (23%)
  matrix products  24.2 us (7%)
  other arithmetic  23.6 us (7%)
  local copies, waits for them, and re-layouts  10.7 us (3%)
  starting transfers between devices  8.13 us (2%)
  between operations  5.93 us (2%)
    ppermute x2, waiting for transfers between devices, from_behind(): return lax.ppermute(block, axis, route)  82.6 us
    psum x1, blocking collectives, per_device(): alpha_value = lax.psum(jnp.sum(vector * image), ('left', 'right')) / entries  75.6 us
    psum x1, blocking collectives, per_device(): start_sum = lax.psum(jnp.sum(masked * masked), ('left', 'right'))  68.7 us
    psum x1, blocking collectives, per_device(): lax.psum(jnp.sum(residual * residual), ('left', 'right')) / entries + 1e-06  62.8 us
    dot_general x1, matrix products, per_device(): jnp.dot(left_env[1, 0], part_one, preferred_element_type=jnp.float32)  14.2 us
    unnamed x4, local copies, waits for them, and re-layouts  10.7 us
    dot_general x1, matrix products, per_device(): jnp.dot(left_env[0, 0], part_zero, preferred_element_type=jnp.float32)  10 us
    ppermute x2, starting transfers between devices, from_behind(): return lax.ppermute(block, axis, route)  8.13 us
  transfers between devices with their start and end apart: 2, of which 2 were waited for; matrix products, arithmetic and copies ran while one was open for 0% of the time, Pallas kernels for 0%

commit v1 on v0

v1 whole, which is shorter than its diff:
```python
import jax
import jax.numpy as jnp
from jax import lax
from jax.experimental import pallas as pl
from jax.experimental.pallas import tpu as pltpu
from jax.sharding import PartitionSpec as P

MESH = pl.DeviceIdType.MESH
BLOCK = 256
PAIR = 4
SEC = 1024
DEVICES = 128
CHUNK = 32
CHUNKS = SEC // CHUNK
MERGED_UP = 13
LOAD = 128
LOADS = SEC // LOAD
TILE = 256
TILES = SEC // TILE
PHASES = ((1, 16), (16, 8))


def own_block():
    return lax.axis_index("left") * 16 + lax.axis_index("right")


def place(block):
    block = lax.rem(block + DEVICES, DEVICES)
    return (lax.div(block, 16), lax.rem(block, 16))


def along_z(block, step, core):
    z = lax.rem(lax.div(block, 2), 4)
    return lax.div(block, 8) * 8 + lax.rem(z + step + 4, 4) * 2 + core


def group_peer(block, stride, size, step):
    digit = lax.rem(lax.div(block, stride), size)
    return block + (lax.rem(digit + step, size) - digit) * stride


def goes_up(chunk):
    return lax.div((chunk + 1) * MERGED_UP, CHUNKS) > lax.div(chunk * MERGED_UP, CHUNKS)


def step_kernel(
    site_ops, left_live, right_live, state, left_env, right_env,
    image, masked, sums,
    own, first, second, source, left_zero, left_one, right_zero, right_one, part,
    slots, share, load_sem, env_sem, first_sem, second_sem, source_sem, send_sem, sum_send, sum_recv,
):
    k = own_block()
    core = lax.rem(k, 2)
    is_low = core == 0
    is_high = core == 1

    loads = [
        pltpu.make_async_copy(
            state.at[0, pl.ds(i * LOAD, LOAD)], masked.at[pl.ds(i * LOAD, LOAD)], load_sem.at[i]
        )
        for i in range(LOADS)
    ]
    for load in loads:
        load.start()
    envs = [
        pltpu.make_async_copy(right_env.at[1, 0], right_one, env_sem.at[0]),
        pltpu.make_async_copy(left_env.at[1, 0], left_one, env_sem.at[1]),
        pltpu.make_async_copy(right_env.at[0, 0], right_zero, env_sem.at[2]),
        pltpu.make_async_copy(left_env.at[0, 0], left_zero, env_sem.at[3]),
    ]
    for env in envs:
        env.start()

    barrier = pltpu.get_barrier_semaphore()

    def greet(block):
        pl.semaphore_signal(barrier, inc=1, device_id=place(block), device_id_type=MESH)

    relay = along_z(k, -1, 0)
    onward = along_z(k, 1, 1) + 3
    @pl.when(is_low)
    def _():
        greet(k - 1)
        greet(k - 2)
        greet(along_z(k, 1, 1))
        greet(along_z(k - 3 + DEVICES, -1, 0))

    @pl.when(is_high)
    def _():
        greet(k - 1)
        greet(k + 1)
        greet(k - 2)

    partners = 0
    for stride, size in PHASES:
        for step in range(1, size):
            greet(group_peer(k, stride, size, step))
            partners += 1

    def weight(target, distance):
        target = lax.rem(target + DEVICES, DEVICES)
        pair = lax.rem(target, PAIR)
        entry = site_ops[0, pair, lax.rem(pair - distance + PAIR, PAIR)]
        return jnp.where(target >= distance, entry, 0.0)

    up_two = weight(k + 2, 2)
    up_three = weight(k + 2, 3)
    merge_own = jnp.where(is_low, up_two, weight(k + 3, 3))
    merge_other = jnp.where(is_low, up_three, weight(k + 3, 2))
    own_pair = lax.rem(k, PAIR)
    diagonal = site_ops[1, own_pair, own_pair]
    sector = lax.div(k, PAIR)
    rows = left_live[sector] * BLOCK
    columns = right_live[sector + lax.div(own_pair + 1, 2)] * BLOCK
    column_live = lax.broadcasted_iota(jnp.int32, (1, SEC), 1) < columns

    def live(first_row, count):
        return (
            lax.broadcasted_iota(jnp.int32, (count, 1), 0) + first_row < rows
        ) & column_live

    def chunk_of(ref, chunk):
        return ref.at[pl.ds(pl.multiple_of(chunk * CHUNK, CHUNK), CHUNK)]

    def send(src, dst, send_at, recv, chunk, target):
        pltpu.make_async_remote_copy(
            src_ref=chunk_of(src, chunk),
            dst_ref=chunk_of(dst, chunk),
            send_sem=send_sem.at[send_at],
            recv_sem=recv.at[chunk],
            device_id=place(target),
            device_id_type=MESH,
        ).start()

    def arrived(ref, recv, chunk):
        pltpu.make_async_copy(chunk_of(ref, chunk), chunk_of(ref, chunk), recv.at[chunk]).wait()

    def fold(values):
        return jnp.sum(values.reshape(-1, 8, SEC // 128, 128), axis=(0, 2))

    share[...] = jnp.zeros_like(share)
    for i in range(LOADS):
        loads[i].wait()
        at = pl.ds(i * LOAD, LOAD)
        values = jnp.where(live(i * LOAD, LOAD), masked[at], 0.0)
        masked[at] = values
        own[at] = values.astype(jnp.bfloat16)
        share[0] += jnp.sum((values * values).reshape(LOAD // 8, 8, SEC), axis=0)
        if i == 0:
            pl.semaphore_wait(barrier, 4 - core + partners)

        @pl.loop(i * (LOAD // CHUNK), (i + 1) * (LOAD // CHUNK))
        def _(chunk):
            @pl.when(is_low)
            def _():
                send(own, first, 0, first_sem, chunk, k + 1)

                @pl.when(jnp.logical_not(goes_up(chunk)))
                def _():
                    send(own, second, 1, second_sem, chunk, k - 1)

            @pl.when(is_high & goes_up(chunk))
            def _():
                send(own, second, 1, second_sem, chunk, k + 1)

    @pl.when(is_high)
    def _():
        @pl.loop(0, CHUNKS)
        def _(chunk):
            arrived(first, first_sem, chunk)
            at = pl.ds(pl.multiple_of(chunk * CHUNK, CHUNK), CHUNK)
            first[at] = (
                up_two * own[at].astype(jnp.float32) + up_three * first[at].astype(jnp.float32)
            ).astype(jnp.bfloat16)
            send(first, source, 2, source_sem, chunk, k + 2)

    def tile_at(index):
        return pl.ds(pl.multiple_of(index * TILE, TILE), TILE)

    def part_one(index):
        at = tile_at(index)
        part[at] = jnp.dot(
            own[at], right_one[...], preferred_element_type=jnp.float32
        ).astype(jnp.bfloat16)

    def image_one(index):
        at = tile_at(index)
        image[at] = diagonal * jnp.dot(left_one[at], part[...], preferred_element_type=jnp.float32)

    def exchange(chunk):
        up = goes_up(chunk)

        @pl.when(up == is_low)
        def _():
            arrived(second, second_sem, chunk)
            at = pl.ds(pl.multiple_of(chunk * CHUNK, CHUNK), CHUNK)
            second[at] = (
                merge_own * own[at].astype(jnp.float32)
                + merge_other * second[at].astype(jnp.float32)
            ).astype(jnp.bfloat16)

            @pl.when(is_low)
            def _():
                send(second, source, 2, source_sem, chunk, k + 2)

            @pl.when(is_high)
            def _():
                send(second, first, 3, first_sem, chunk, relay)

        @pl.when(is_low & jnp.logical_not(up))
        def _():
            arrived(first, first_sem, chunk)
            send(first, source, 3, source_sem, chunk, onward)

    @pl.loop(0, TILES)
    def _(index):
        @pl.when(index == 0)
        def _():
            envs[0].wait()
            envs[1].wait()
            envs[2].wait()
            envs[3].wait()

        part_one(index)
        exchange(2 * index)
        exchange(2 * index + 1)

    @pl.loop(0, TILES)
    def _(index):
        image_one(index)
        exchange(2 * index + 8)
        exchange(2 * index + 9)

    per_tile = TILE // CHUNK

    def consume(index, last):
        @pl.loop(index * per_tile, (index + 1) * per_tile)
        def _(chunk):
            arrived(source, source_sem, chunk)

        piece = pl.ds(index * TILE, TILE)
        part[piece] = jnp.dot(
            source[piece], right_zero[...], preferred_element_type=jnp.float32
        ).astype(jnp.bfloat16)

        @pl.loop(0, TILES)
        def _(row):
            at = tile_at(row)
            values = image[at] + jnp.dot(
                left_zero[at, piece], part[piece], preferred_element_type=jnp.float32
            )
            if last:
                values = jnp.where(live(row * TILE, TILE), values, 0.0)
                share[1] += jnp.sum((values * masked[at]).reshape(TILE // 8, 8, SEC), axis=0)
                share[2] += jnp.sum((values * values).reshape(TILE // 8, 8, SEC), axis=0)
            image[at] = values

    consume(0, False)

    @pl.loop(16, 24)
    def _(chunk):
        exchange(chunk)

    consume(1, False)

    @pl.loop(24, 32)
    def _(chunk):
        exchange(chunk)

    consume(2, False)
    consume(3, True)

    for phase, (stride, size) in enumerate(PHASES):
        digit = lax.rem(lax.div(k, stride), size)
        if phase == 0:
            total = jnp.sum(share[...].reshape(3, 8, SEC // 128, 128), axis=2)
        else:
            total = jnp.sum(slots[phase - 1, 0 : PHASES[phase - 1][1]], axis=0)
        slots[phase, digit] = total
        for step in range(1, size):
            pltpu.make_async_remote_copy(
                src_ref=slots.at[phase, digit],
                dst_ref=slots.at[phase, digit],
                send_sem=sum_send.at[phase],
                recv_sem=sum_recv.at[phase],
                device_id=place(group_peer(k, stride, size, step)),
                device_id_type=MESH,
            ).start()
        others = slots.at[phase, pl.ds(0, size - 1)]
        pltpu.make_async_copy(others, others, sum_recv.at[phase]).wait()
        pltpu.make_async_copy(others, others, sum_send.at[phase]).wait()
    total = jnp.sum(slots[len(PHASES) - 1, 0 : PHASES[-1][1]], axis=0)
    total = jnp.sum(jnp.sum(total, axis=2, keepdims=True), axis=1, keepdims=True)
    entries = float(DEVICES * SEC * SEC)
    start = total[0] / entries
    overlap = total[1] / entries
    square = total[2] / entries
    scale = 1.0 / jnp.sqrt(start + 1e-06)
    slope = scale * scale * overlap
    rest = square - 2.0 * slope * overlap + slope * slope * start
    beta = jnp.sqrt(scale * scale * jnp.maximum(rest, 0.0) + 1e-06)
    sums[0] = jnp.broadcast_to(slope, (8, 128))
    sums[1] = jnp.broadcast_to(scale / beta, (8, 128))
    sums[2] = jnp.broadcast_to(beta, (8, 128))

    def sent(flow, chunks):
        piece = own.at[pl.ds(0, chunks * CHUNK)]
        pltpu.make_async_copy(piece, piece, send_sem.at[flow]).wait()

    @pl.when(is_low)
    def _():
        sent(0, CHUNKS)
        sent(1, CHUNKS - MERGED_UP)
        sent(2, MERGED_UP)
        sent(3, CHUNKS - MERGED_UP)

    @pl.when(is_high)
    def _():
        sent(1, MERGED_UP)
        sent(2, CHUNKS)
        sent(3, CHUNKS - MERGED_UP)


def finish_kernel(sums, image, masked, next_vector, coefficients):
    slope = sums[0, 0:1, 0:1]
    gain = sums[1, 0:1, 0:1]
    next_vector[0] = (image[...] - slope * masked[...]) * gain
    coefficients[0] = jnp.max(sums[0])
    coefficients[1] = jnp.max(sums[2])


def per_device(state, left_env, right_env, site_ops, left_live, right_live):
    hbm = pl.BlockSpec(memory_space=pltpu.HBM)
    smem = pl.BlockSpec(memory_space=pltpu.SMEM)
    vmem = pl.BlockSpec(memory_space=pltpu.VMEM)
    block = pltpu.VMEM((SEC, SEC), jnp.bfloat16)
    dma = pltpu.SemaphoreType.DMA
    image, masked, sums = pl.pallas_call(
        step_kernel,
        out_shape=(
            jax.ShapeDtypeStruct((SEC, SEC), jnp.float32),
            jax.ShapeDtypeStruct((SEC, SEC), jnp.float32),
            jax.ShapeDtypeStruct((3, 8, 128), jnp.float32),
        ),
        in_specs=[smem, smem, smem, hbm, hbm, hbm],
        out_specs=(vmem, vmem, vmem),
        scratch_shapes=[
            block, block, block, block, block, block, block, block, block,
            pltpu.VMEM((len(PHASES), max(size for _, size in PHASES), 3, 8, 128), jnp.float32),
            pltpu.VMEM((3, 8, SEC), jnp.float32),
            dma((LOADS,)), dma((4,)), dma((CHUNKS,)), dma((CHUNKS,)), dma((CHUNKS,)), dma((4,)),
            dma((len(PHASES),)), dma((len(PHASES),)),
        ],
        compiler_params=pltpu.CompilerParams(
            collective_id=0, has_side_effects=True, vmem_limit_bytes=44 * 1024 * 1024
        ),
        cost_estimate=pl.CostEstimate(flops=8 * SEC**3, bytes_accessed=20 << 20, transcendentals=0),
    )(site_ops, left_live, right_live, state, left_env, right_env)
    return pl.pallas_call(
        finish_kernel,
        grid=(8,),
        out_shape=(
            jax.ShapeDtypeStruct((1, SEC, SEC), jnp.float32),
            jax.ShapeDtypeStruct((2,), jnp.float32),
        ),
        in_specs=[
            pl.BlockSpec((3, 8, 128), lambda i: (0, 0, 0)),
            pl.BlockSpec((SEC // 8, SEC), lambda i: (i, 0)),
            pl.BlockSpec((SEC // 8, SEC), lambda i: (i, 0)),
        ],
        out_specs=(pl.BlockSpec((1, SEC // 8, SEC), lambda i: (0, i, 0)), smem),
        cost_estimate=pl.CostEstimate(flops=3 * SEC**2, bytes_accessed=12 << 20, transcendentals=0),
    )(sums, image, masked)


def solution(mesh):
    in_specs = (
        P(("left", "right"), None, None),
        P(None, ("left", "right"), None, None),
        P(None, ("left", "right"), None, None),
        P(),
        P(),
        P(),
    )
    out_specs = (P(("left", "right"), None, None), P())
    return jax.shard_map(
        per_device, mesh=mesh, in_specs=in_specs, out_specs=out_specs, check_vma=False
    )
```

time: 363 us -> 84 us (0.23)
  blocking collectives: 207 us -> 0 us
  waiting for transfers between devices: 82.6 us -> 0 us
  Pallas kernels: 0 us -> 76.6 us
  matrix products: 24.2 us -> 0 us
  other arithmetic: 23.6 us -> 0 us
  starting transfers between devices: 8.13 us -> 0 us
  between operations: 5.93 us -> 0.66 us
  local copies, waits for them, and re-layouts: 10.7 us -> 6.49 us
    psum x3 -> x0, blocking collectives: 207 us -> none  [the longest x1 75.6 us: per_device(): alpha_value = lax.psum(jnp.sum(vector * image), ('left', 'right')) / entries]
    ppermute x2 -> x0, waiting for transfers between devices: 82.6 us -> none  [from_behind(): return lax.ppermute(block, axis, route)]
    pallas_call x0 -> x2, Pallas kernels: none -> 76.6 us  [the longest x1 68.6 us: per_device(): pl.pallas_call(step_kernel, out_shape=(jax.ShapeDtypeStruct((SEC, SEC), j...]
    dot_general x2 -> x0, matrix products: 24.2 us -> none  [the longest x1 14.2 us: per_device(): jnp.dot(left_env[1, 0], part_one, preferred_element_type=jnp.float32)]
    reduce_sum x6 -> x0, other arithmetic: 13.9 us -> none  [the longest x1 5.74 us: per_device(): jnp.sum(residual * residual)]
    ppermute x2 -> x0, starting transfers between devices: 8.13 us -> none  [from_behind(): return lax.ppermute(block, axis, route)]
    broadcast_in_dim x1 -> x0, other arithmetic: 6.39 us -> none  [per_device(): return (next_vector[None], jnp.stack([alpha_value, beta_value]))]
    unnamed x4 -> x12, local copies, waits for them, and re-layouts: 10.7 us -> 6.49 us
  transfers between devices with their start and end apart: 2 -> 0, of which waited for: 2 -> 0; matrix products, arithmetic and copies ran while one was open for 0% -> 0% of each run, Pallas kernels for 0% -> 0%
where the time goes in v1:
time: 84 us; the launch traced here: 83.7 us
  Pallas kernels  76.6 us (91%)
  local copies, waits for them, and re-layouts  6.49 us (8%)
    pallas_call x1, Pallas kernels, per_device(): pl.pallas_call(step_kernel, out_shape=(jax.ShapeDtypeStruct((SEC, SEC), j...  68.6 us
    pallas_call x1, Pallas kernels, per_device(): pl.pallas_call(finish_kernel, grid=(8,), out_shape=(jax.ShapeDtypeStruct(...  7.94 us
    unnamed x12, local copies, waits for them, and re-layouts  6.49 us

profile of v1, /device:TPU:1, one launch (start us, length us, event | category | flops | bytes accessed | tf_op | source)
XLA Modules:
  0.0 83.7 jit_solution(5242322856398774822)
XLA Ops:
  0.6 0.0 copy-start.3
  0.6 0.7 copy-done.3
  1.3 0.0 copy-start.4
  1.3 0.7 copy-done.4
  2.0 0.0 copy-start.5
  2.0 0.7 copy-done.5
  2.6 68.6 %shard_map.77 = (f32[1024,1024]{1,0:T(8,128)S(1)}, f32[1024,1024]{1,0:T(8,128)S(1)}, f32[3,8,128]{2,1,0:T(8,128)S(1)}) custom-call(f32[2,4,4]{2,1,0:T(4,128)S(1)} %copy-done.3, s32[32]{0:T(128)S(1)} %copy-done.4, s32[34]{0:T(128)S(1)} %copy-done.5, f32[1,1024,1024]{2,1,0:T(8,128)} %state.1, bf16[2,1,1024,1024]{3,2,1,0:T(8,128)(2,1)} %left_env.1, ...), custom_call_target="tpu_custom_call" | custom-call | flops 8589934592 | bytes 20971520 | tf_op jit(solution)/shard_map/pallas_call | solution.py:338
  71.3 0.0 copy-start
  71.3 1.9 %copy-done = f32[1024,1024]{1,0:T(8,128)} copy-done((f32[1024,1024]{1,0:T(8,128)}, f32[1024,1024]{1,0:T(8,128)S(1)}, u32[]{:S(2)}) %copy-start) | copy-done | bytes 4194328
  73.2 0.0 copy-start.1
  73.2 2.0 %copy-done.1 = f32[1024,1024]{1,0:T(8,128)} copy-done((f32[1024,1024]{1,0:T(8,128)}, f32[1024,1024]{1,0:T(8,128)S(1)}, u32[]{:S(2)}) %copy-start.1) | copy-done | bytes 4194328
  75.2 0.0 copy-start.2
  75.2 0.6 copy-done.2
  75.8 7.9 %shard_map.78 = (f32[1,1024,1024]{2,1,0:T(8,128)}, f32[2]{0:T(128)}) custom-call(f32[3,8,128]{2,1,0:T(8,128)} %copy-done.2, f32[1024,1024]{1,0:T(8,128)} %copy-done, f32[1024,1024]{1,0:T(8,128)} %copy-done.1), custom_call_target="tpu_custom_call" | custom-call | flops 3145728 | bytes 12582912 | tf_op jit(solution)/shard_map/pallas_call | solution.py:359
Async XLA Ops:
  0.6 0.7 copy-start.3
  1.3 0.7 copy-start.4
  2.0 0.7 copy-start.5
  71.3 1.9 %copy-start = (f32[1024,1024]{1,0:T(8,128)}, f32[1024,1024]{1,0:T(8,128)S(1)}, u32[]{:S(2)}) copy-start(f32[1024,1024]{1,0:T(8,128)S(1)} %get-tuple-element.6.image) | copy-start | bytes 12582916
  73.2 2.0 %copy-start.1 = (f32[1024,1024]{1,0:T(8,128)}, f32[1024,1024]{1,0:T(8,128)S(1)}, u32[]{:S(2)}) copy-start(f32[1024,1024]{1,0:T(8,128)S(1)} %get-tuple-element.7.masked) | copy-start | bytes 12582916
  75.2 0.6 copy-start.2

commit v2 on v1

--- a/solution.py
+++ b/solution.py
@@ -17,7 +17,8 @@
 LOADS = SEC // LOAD
 TILE = 256
 TILES = SEC // TILE
-PHASES = ((1, 16), (16, 8))
+PHASES = ((1, 8), (8, 16))
+ROUNDS = 3
 
 
 def own_block():
@@ -39,21 +40,48 @@
     return block + (lax.rem(digit + step, size) - digit) * stride
 
 
+def axis_distance(step, size):
+    return min(step % size, size - step % size)
+
+
+def phase_steps(phase):
+    inner = 2 if phase == 0 else 4
+    size = PHASES[phase][1]
+    outer = size // inner
+    steps = [(a, b) for a in range(outer) for b in range(inner) if a or b]
+    return sorted(steps, key=lambda s: -(axis_distance(s[0], outer) + axis_distance(s[1], inner)))
+
+
+def phase_peer(block, phase, step):
+    inner = 2 if phase == 0 else 4
+    stride, size = PHASES[phase]
+    block = group_peer(block, stride, inner, step[1])
+    return group_peer(block, stride * inner, size // inner, step[0])
+
+
 def goes_up(chunk):
     return lax.div((chunk + 1) * MERGED_UP, CHUNKS) > lax.div(chunk * MERGED_UP, CHUNKS)
 
 
 def step_kernel(
-    site_ops, left_live, right_live, state, left_env, right_env,
+    site_hbm, left_hbm, right_hbm, state, left_env, right_env,
     image, masked, sums,
+    site_ops, left_live, right_live,
     own, first, second, source, left_zero, left_one, right_zero, right_one, part,
-    slots, share, load_sem, env_sem, first_sem, second_sem, source_sem, send_sem, sum_send, sum_recv,
+    slots, share, small_sem, load_sem, env_sem, first_sem, second_sem, source_sem, send_sem, sum_send, sum_recv, near_sem,
 ):
     k = own_block()
     core = lax.rem(k, 2)
     is_low = core == 0
     is_high = core == 1
 
+    small = [
+        pltpu.make_async_copy(site_hbm, site_ops, small_sem.at[0]),
+        pltpu.make_async_copy(left_hbm, left_live, small_sem.at[1]),
+        pltpu.make_async_copy(right_hbm, right_live, small_sem.at[2]),
+    ]
+    for copy in small:
+        copy.start()
     loads = [
         pltpu.make_async_copy(
             state.at[0, pl.ds(i * LOAD, LOAD)], masked.at[pl.ds(i * LOAD, LOAD)], load_sem.at[i]
@@ -68,34 +96,46 @@
         pltpu.make_async_copy(right_env.at[0, 0], right_zero, env_sem.at[2]),
         pltpu.make_async_copy(left_env.at[0, 0], left_zero, env_sem.at[3]),
     ]
+
+    barrier = pltpu.get_barrier_semaphore()
+
+    def greet(block):
+        pl.semaphore_signal(barrier, inc=1, device_id=place(block), device_id_type=MESH)
+
+    def relay_of(merger):
+        z = lax.rem(lax.div(merger, 2), 4)
+        crossed = along_z(lax.rem(merger + 3, DEVICES), 1, 0)
+        return jnp.where(z == 2, crossed, along_z(merger, -1, 0))
+
+    z = lax.rem(lax.div(k, 2), 4)
+    relay = relay_of(k)
+    crossing = lax.rem(along_z(k, -1, 0) + DEVICES - 3, DEVICES)
+    merger = jnp.where(z == 1, crossing, along_z(k, 1, 1))
+    onward = merger + 3
+    near = [
+        along_z(k, 1, core), along_z(k, -1, core), group_peer(k, 1, 2, 1),
+        group_peer(k, 8, 4, 1), group_peer(k, 8, 4, 3), group_peer(k, 32, 4, 1), group_peer(k, 32, 4, 3),
+    ]
+
+    greet(k - 1)
+    greet(k - 2)
+
+    @pl.when(is_low)
+    def _():
+        greet(merger)
+        greet(relay_of(lax.rem(k - 3 + DEVICES, DEVICES)))
+
+    @pl.when(is_high)
+    def _():
+        greet(k + 1)
+
+    for block in near:
+        greet(block)
     for env in envs:
         env.start()
 
-    barrier = pltpu.get_barrier_semaphore()
-
-    def greet(block):
-        pl.semaphore_signal(barrier, inc=1, device_id=place(block), device_id_type=MESH)
-
-    relay = along_z(k, -1, 0)
-    onward = along_z(k, 1, 1) + 3
-    @pl.when(is_low)
-    def _():
-        greet(k - 1)
-        greet(k - 2)
-        greet(along_z(k, 1, 1))
-        greet(along_z(k - 3 + DEVICES, -1, 0))
-
-    @pl.when(is_high)
-    def _():
-        greet(k - 1)
-        greet(k + 1)
-        greet(k - 2)
-
-    partners = 0
-    for stride, size in PHASES:
-        for step in range(1, size):
-            greet(group_peer(k, stride, size, step))
-            partners += 1
+    for copy in small:
+        copy.wait()
 
     def weight(target, distance):
         target = lax.rem(target + DEVICES, DEVICES)
@@ -147,7 +187,7 @@
         own[at] = values.astype(jnp.bfloat16)
         share[0] += jnp.sum((values * values).reshape(LOAD // 8, 8, SEC), axis=0)
         if i == 0:
-            pl.semaphore_wait(barrier, 4 - core + partners)
+            pl.semaphore_wait(barrier, 4 - core + len(near))
 
         @pl.loop(i * (LOAD // CHUNK), (i + 1) * (LOAD // CHUNK))
         def _(chunk):
@@ -163,32 +203,30 @@
             def _():
                 send(own, second, 1, second_sem, chunk, k + 1)
 
-    @pl.when(is_high)
-    def _():
-        @pl.loop(0, CHUNKS)
-        def _(chunk):
+    def tile_at(index):
+        return pl.ds(pl.multiple_of(index * TILE, TILE), TILE)
+
+    def part_one(index):
+        at = tile_at(index)
+        part[at] = jnp.dot(
+            own[at], right_one[...], preferred_element_type=jnp.float32
+        ).astype(jnp.bfloat16)
+
+    def image_one(index):
+        at = tile_at(index)
+        image[at] = diagonal * jnp.dot(left_one[at], part[...], preferred_element_type=jnp.float32)
+
+    def exchange(chunk):
+        up = goes_up(chunk)
+
+        @pl.when(is_high)
+        def _():
             arrived(first, first_sem, chunk)
             at = pl.ds(pl.multiple_of(chunk * CHUNK, CHUNK), CHUNK)
             first[at] = (
                 up_two * own[at].astype(jnp.float32) + up_three * first[at].astype(jnp.float32)
             ).astype(jnp.bfloat16)
             send(first, source, 2, source_sem, chunk, k + 2)
-
-    def tile_at(index):
-        return pl.ds(pl.multiple_of(index * TILE, TILE), TILE)
-
-    def part_one(index):
-        at = tile_at(index)
-        part[at] = jnp.dot(
-            own[at], right_one[...], preferred_element_type=jnp.float32
-        ).astype(jnp.bfloat16)
-
-    def image_one(index):
-        at = tile_at(index)
-        image[at] = diagonal * jnp.dot(left_one[at], part[...], preferred_element_type=jnp.float32)
-
-    def exchange(chunk):
-        up = goes_up(chunk)
 
         @pl.when(up == is_low)
         def _():
@@ -212,6 +250,17 @@
             arrived(first, first_sem, chunk)
             send(first, source, 3, source_sem, chunk, onward)
 
+    def tell(round_sem):
+        for block in near:
+            pl.semaphore_signal(
+                near_sem.at[round_sem], inc=1, device_id=place(block), device_id_type=MESH
+            )
+
+    def told(round_sem):
+        pl.semaphore_wait(near_sem.at[round_sem], len(near))
+
+    tell(0)
+
     @pl.loop(0, TILES)
     def _(index):
         @pl.when(index == 0)
@@ -224,6 +273,9 @@
         part_one(index)
         exchange(2 * index)
         exchange(2 * index + 1)
+
+    told(0)
+    tell(1)
 
     @pl.loop(0, TILES)
     def _(index):
@@ -255,6 +307,8 @@
                 share[2] += jnp.sum((values * values).reshape(TILE // 8, 8, SEC), axis=0)
             image[at] = values
 
+    told(1)
+    tell(2)
     consume(0, False)
 
     @pl.loop(16, 24)
@@ -267,6 +321,7 @@
     def _(chunk):
         exchange(chunk)
 
+    told(2)
     consume(2, False)
     consume(3, True)
 
@@ -277,18 +332,17 @@
         else:
             total = jnp.sum(slots[phase - 1, 0 : PHASES[phase - 1][1]], axis=0)
         slots[phase, digit] = total
-        for step in range(1, size):
+        for step in phase_steps(phase):
             pltpu.make_async_remote_copy(
                 src_ref=slots.at[phase, digit],
                 dst_ref=slots.at[phase, digit],
                 send_sem=sum_send.at[phase],
                 recv_sem=sum_recv.at[phase],
-                device_id=place(group_peer(k, stride, size, step)),
+                device_id=place(phase_peer(k, phase, step)),
                 device_id_type=MESH,
             ).start()
         others = slots.at[phase, pl.ds(0, size - 1)]
         pltpu.make_async_copy(others, others, sum_recv.at[phase]).wait()
-        pltpu.make_async_copy(others, others, sum_send.at[phase]).wait()
     total = jnp.sum(slots[len(PHASES) - 1, 0 : PHASES[-1][1]], axis=0)
     total = jnp.sum(jnp.sum(total, axis=2, keepdims=True), axis=1, keepdims=True)
     entries = float(DEVICES * SEC * SEC)
@@ -303,6 +357,10 @@
     sums[1] = jnp.broadcast_to(scale / beta, (8, 128))
     sums[2] = jnp.broadcast_to(beta, (8, 128))
 
+    for phase, (stride, size) in enumerate(PHASES):
+        others = slots.at[phase, pl.ds(0, size - 1)]
+        pltpu.make_async_copy(others, others, sum_send.at[phase]).wait()
+
     def sent(flow, chunks):
         piece = own.at[pl.ds(0, chunks * CHUNK)]
         pltpu.make_async_copy(piece, piece, send_sem.at[flow]).wait()
@@ -321,12 +379,20 @@
         sent(3, CHUNKS - MERGED_UP)
 
 
-def finish_kernel(sums, image, masked, next_vector, coefficients):
+def finish_kernel(sums, image, masked, next_vector, coefficients, result, sem):
     slope = sums[0, 0:1, 0:1]
     gain = sums[1, 0:1, 0:1]
-    next_vector[0] = (image[...] - slope * masked[...]) * gain
+    copies = []
+    for i in range(LOADS):
+        at = pl.ds(i * LOAD, LOAD)
+        result[at] = (image[at] - slope * masked[at]) * gain
+        copy = pltpu.make_async_copy(result.at[at], next_vector.at[0, at], sem.at[i])
+        copy.start()
+        copies.append(copy)
     coefficients[0] = jnp.max(sums[0])
     coefficients[1] = jnp.max(sums[2])
+    for copy in copies:
+        copy.wait()
 
 
 def per_device(state, left_env, right_env, site_ops, left_live, right_live):
@@ -335,6 +401,10 @@
     vmem = pl.BlockSpec(memory_space=pltpu.VMEM)
     block = pltpu.VMEM((SEC, SEC), jnp.bfloat16)
     dma = pltpu.SemaphoreType.DMA
+    state, left_env, right_env, site_ops, left_live, right_live = (
+        pltpu.with_memory_space_constraint(array, pltpu.HBM)
+        for array in (state, left_env, right_env, site_ops, left_live, right_live)
+    )
     image, masked, sums = pl.pallas_call(
         step_kernel,
         out_shape=(
@@ -342,14 +412,18 @@
             jax.ShapeDtypeStruct((SEC, SEC), jnp.float32),
             jax.ShapeDtypeStruct((3, 8, 128), jnp.float32),
         ),
-        in_specs=[smem, smem, smem, hbm, hbm, hbm],
+        in_specs=[hbm] * 6,
         out_specs=(vmem, vmem, vmem),
         scratch_shapes=[
+            pltpu.SMEM(site_ops.shape, jnp.float32),
+            pltpu.SMEM(left_live.shape, jnp.int32),
+            pltpu.SMEM(right_live.shape, jnp.int32),
             block, block, block, block, block, block, block, block, block,
             pltpu.VMEM((len(PHASES), max(size for _, size in PHASES), 3, 8, 128), jnp.float32),
             pltpu.VMEM((3, 8, SEC), jnp.float32),
-            dma((LOADS,)), dma((4,)), dma((CHUNKS,)), dma((CHUNKS,)), dma((CHUNKS,)), dma((4,)),
+            dma((3,)), dma((LOADS,)), dma((4,)), dma((CHUNKS,)), dma((CHUNKS,)), dma((CHUNKS,)), dma((4,)),
             dma((len(PHASES),)), dma((len(PHASES),)),
+            pltpu.SemaphoreType.REGULAR((ROUNDS,)),
         ],
         compiler_params=pltpu.CompilerParams(
             collective_id=0, has_side_effects=True, vmem_limit_bytes=44 * 1024 * 1024
@@ -358,18 +432,15 @@
     )(site_ops, left_live, right_live, state, left_env, right_env)
     return pl.pallas_call(
         finish_kernel,
-        grid=(8,),
         out_shape=(
             jax.ShapeDtypeStruct((1, SEC, SEC), jnp.float32),
             jax.ShapeDtypeStruct((2,), jnp.float32),
         ),
-        in_specs=[
-            pl.BlockSpec((3, 8, 128), lambda i: (0, 0, 0)),
-            pl.BlockSpec((SEC // 8, SEC), lambda i: (i, 0)),
-            pl.BlockSpec((SEC // 8, SEC), lambda i: (i, 0)),
-        ],
-        out_specs=(pl.BlockSpec((1, SEC // 8, SEC), lambda i: (0, i, 0)), smem),
-        cost_estimate=pl.CostEstimate(flops=3 * SEC**2, bytes_accessed=12 << 20, transcendentals=0),
+        in_specs=[vmem, vmem, vmem],
+        out_specs=(hbm, smem),
+        scratch_shapes=[pltpu.VMEM((SEC, SEC), jnp.float32), dma((LOADS,))],
+        compiler_params=pltpu.CompilerParams(vmem_limit_bytes=16 * 1024 * 1024),
+        cost_estimate=pl.CostEstimate(flops=3 * SEC**2, bytes_accessed=4 << 20, transcendentals=0),
     )(sums, image, masked)
 
 

time: 84 us -> 69.1 us (0.82)
  Pallas kernels: 76.6 us -> 68.2 us
  local copies, waits for them, and re-layouts: 6.49 us -> 0 us
    unnamed x12 -> x0, local copies, waits for them, and re-layouts: 6.49 us -> none
    pallas_call x1, Pallas kernels: 7.94 us -> 2.73 us  [per_device(): pl.pallas_call(finish_kernel, out_shape=(jax.ShapeDtypeStruct((1, SEC, SE...]
    pallas_call x1, Pallas kernels: 68.6 us -> 65.5 us  [per_device(): pl.pallas_call(step_kernel, out_shape=(jax.ShapeDtypeStruct((SEC, SEC), j...]
where the time goes in v2:
time: 69.1 us; the launch traced here: 68.8 us
  Pallas kernels  68.2 us (99%)
    pallas_call x1, Pallas kernels, per_device(): pl.pallas_call(step_kernel, out_shape=(jax.ShapeDtypeStruct((SEC, SEC), j...  65.5 us
    pallas_call x1, Pallas kernels, per_device(): pl.pallas_call(finish_kernel, out_shape=(jax.ShapeDtypeStruct((1, SEC, SE...  2.73 us

profile of v2, /device:TPU:1, one launch (start us, length us, event | category | flops | bytes accessed | tf_op | source)
XLA Modules:
  0.0 68.8 jit_solution(1078328942108465236)
XLA Ops:
  0.6 65.5 %shard_map.77 = (f32[1024,1024]{1,0:T(8,128)S(1)}, f32[1024,1024]{1,0:T(8,128)S(1)}, f32[3,8,128]{2,1,0:T(8,128)S(1)}) custom-call(f32[2,4,4]{2,1,0:T(4,128)} %site_hbm.1, s32[32]{0:T(128)} %left_hbm.1, s32[34]{0:T(128)} %right_hbm.1, f32[1,1024,1024]{2,1,0:T(8,128)} %state.1, bf16[2,1,1024,1024]{3,2,1,0:T(8,128)(2,1)} %left_env.1, ...), custom_call_target="tpu_custom_call" | custom-call | flops 8589934592 | bytes 20971520 | tf_op jit(solution)/shard_map/pallas_call | solution.py:408
  66.1 2.7 %shard_map.78 = (f32[1,1024,1024]{2,1,0:T(8,128)}, f32[2]{0:T(128)}) custom-call(f32[3,8,128]{2,1,0:T(8,128)S(1)} %get-tuple-element.5.sums, f32[1024,1024]{1,0:T(8,128)S(1)} %get-tuple-element.6.image, f32[1024,1024]{1,0:T(8,128)S(1)} %get-tuple-element.7.masked), custom_call_target="tpu_custom_call" | custom-call | flops 3145728 | bytes 4194304 | tf_op jit(solution)/shard_map/pallas_call | solution.py:433

commit v3 on v2

--- a/solution.py
+++ b/solution.py
@@ -12,9 +12,10 @@
 DEVICES = 128
 CHUNK = 32
 CHUNKS = SEC // CHUNK
-MERGED_UP = 13
+MERGED_UP = (13, 13, 15, 15)
 LOAD = 128
 LOADS = SEC // LOAD
+OUT = 64
 TILE = 256
 TILES = SEC // TILE
 PHASES = ((1, 8), (8, 16))
@@ -59,8 +60,16 @@
     return group_peer(block, stride * inner, size // inner, step[0])
 
 
-def goes_up(chunk):
-    return lax.div((chunk + 1) * MERGED_UP, CHUNKS) > lax.div(chunk * MERGED_UP, CHUNKS)
+def target_z(target):
+    return lax.rem(lax.div(lax.rem(target, DEVICES), 2), 4)
+
+
+def goes_up(chunk, target):
+    z = target_z(target)
+    count = jnp.int32(MERGED_UP[0])
+    for i in range(1, 4):
+        count = jnp.where(z == i, MERGED_UP[i], count)
+    return lax.div((chunk + 1) * count, CHUNKS) > lax.div(chunk * count, CHUNKS)
 
 
 def step_kernel(
@@ -74,6 +83,42 @@
     core = lax.rem(k, 2)
     is_low = core == 0
     is_high = core == 1
+
+    barrier = pltpu.get_barrier_semaphore()
+
+    def greet(block):
+        pl.semaphore_signal(barrier, inc=1, device_id=place(block), device_id_type=MESH)
+
+    def relay_of(merger):
+        z = lax.rem(lax.div(merger, 2), 4)
+        crossed = along_z(lax.rem(merger + 3, DEVICES), 1, 0)
+        return jnp.where(z == 2, crossed, along_z(merger, -1, 0))
+
+    z = lax.rem(lax.div(k, 2), 4)
+    relay = relay_of(k)
+    crossing = lax.rem(along_z(k, -1, 0) + DEVICES - 3, DEVICES)
+    merger = jnp.where(z == 1, crossing, along_z(k, 1, 1))
+    onward = lax.rem(merger + 3, DEVICES)
+    target = k + 2 + core
+    near = [
+        along_z(k, 1, core), along_z(k, -1, core), group_peer(k, 1, 2, 1),
+        group_peer(k, 8, 4, 1), group_peer(k, 8, 4, 3), group_peer(k, 32, 4, 1), group_peer(k, 32, 4, 3),
+    ]
+
+    greet(k - 1)
+    greet(k - 2)
+
+    @pl.when(is_low)
+    def _():
+        greet(merger)
+        greet(relay_of(lax.rem(k - 3 + DEVICES, DEVICES)))
+
+    @pl.when(is_high)
+    def _():
+        greet(k + 1)
+
+    for block in near:
+        greet(block)
 
     small = [
         pltpu.make_async_copy(site_hbm, site_ops, small_sem.at[0]),
@@ -97,43 +142,6 @@
         pltpu.make_async_copy(left_env.at[0, 0], left_zero, env_sem.at[3]),
     ]
 
-    barrier = pltpu.get_barrier_semaphore()
-
-    def greet(block):
-        pl.semaphore_signal(barrier, inc=1, device_id=place(block), device_id_type=MESH)
-
-    def relay_of(merger):
-        z = lax.rem(lax.div(merger, 2), 4)
-        crossed = along_z(lax.rem(merger + 3, DEVICES), 1, 0)
-        return jnp.where(z == 2, crossed, along_z(merger, -1, 0))
-
-    z = lax.rem(lax.div(k, 2), 4)
-    relay = relay_of(k)
-    crossing = lax.rem(along_z(k, -1, 0) + DEVICES - 3, DEVICES)
-    merger = jnp.where(z == 1, crossing, along_z(k, 1, 1))
-    onward = merger + 3
-    near = [
-        along_z(k, 1, core), along_z(k, -1, core), group_peer(k, 1, 2, 1),
-        group_peer(k, 8, 4, 1), group_peer(k, 8, 4, 3), group_peer(k, 32, 4, 1), group_peer(k, 32, 4, 3),
-    ]
-
-    greet(k - 1)
-    greet(k - 2)
-
-    @pl.when(is_low)
-    def _():
-        greet(merger)
-        greet(relay_of(lax.rem(k - 3 + DEVICES, DEVICES)))
-
-    @pl.when(is_high)
-    def _():
-        greet(k + 1)
-
-    for block in near:
-        greet(block)
-    for env in envs:
-        env.start()
-
     for copy in small:
         copy.wait()
 
@@ -185,7 +193,9 @@
         values = jnp.where(live(i * LOAD, LOAD), masked[at], 0.0)
         masked[at] = values
         own[at] = values.astype(jnp.bfloat16)
-        share[0] += jnp.sum((values * values).reshape(LOAD // 8, 8, SEC), axis=0)
+        if i == 1:
+            for env in envs:
+                env.start()
         if i == 0:
             pl.semaphore_wait(barrier, 4 - core + len(near))
 
@@ -195,11 +205,11 @@
             def _():
                 send(own, first, 0, first_sem, chunk, k + 1)
 
-                @pl.when(jnp.logical_not(goes_up(chunk)))
+                @pl.when(jnp.logical_not(goes_up(chunk, target)))
                 def _():
                     send(own, second, 1, second_sem, chunk, k - 1)
 
-            @pl.when(is_high & goes_up(chunk))
+            @pl.when(is_high & goes_up(chunk, target))
             def _():
                 send(own, second, 1, second_sem, chunk, k + 1)
 
@@ -208,6 +218,8 @@
 
     def part_one(index):
         at = tile_at(index)
+        values = masked[at]
+        share[0] += jnp.sum((values * values).reshape(TILE // 8, 8, SEC), axis=0)
         part[at] = jnp.dot(
             own[at], right_one[...], preferred_element_type=jnp.float32
         ).astype(jnp.bfloat16)
@@ -217,7 +229,7 @@
         image[at] = diagonal * jnp.dot(left_one[at], part[...], preferred_element_type=jnp.float32)
 
     def exchange(chunk):
-        up = goes_up(chunk)
+        up = goes_up(chunk, target)
 
         @pl.when(is_high)
         def _():
@@ -245,7 +257,7 @@
             def _():
                 send(second, first, 3, first_sem, chunk, relay)
 
-        @pl.when(is_low & jnp.logical_not(up))
+        @pl.when(is_low & jnp.logical_not(goes_up(chunk, onward)))
         def _():
             arrived(first, first_sem, chunk)
             send(first, source, 3, source_sem, chunk, onward)
@@ -260,37 +272,34 @@
         pl.semaphore_wait(near_sem.at[round_sem], len(near))
 
     tell(0)
+    envs[0].wait()
 
     @pl.loop(0, TILES)
     def _(index):
-        @pl.when(index == 0)
-        def _():
-            envs[0].wait()
-            envs[1].wait()
-            envs[2].wait()
-            envs[3].wait()
-
         part_one(index)
-        exchange(2 * index)
-        exchange(2 * index + 1)
+
+        @pl.loop(index * (CHUNKS // 16), (index + 1) * (CHUNKS // 16))
+        def _(chunk):
+            exchange(chunk)
 
     told(0)
     tell(1)
+    envs[1].wait()
 
     @pl.loop(0, TILES)
     def _(index):
         image_one(index)
-        exchange(2 * index + 8)
-        exchange(2 * index + 9)
-
-    per_tile = TILE // CHUNK
-
-    def consume(index, last):
-        @pl.loop(index * per_tile, (index + 1) * per_tile)
+
+        @pl.loop((index + 4) * (CHUNKS // 16), (index + 5) * (CHUNKS // 16))
+        def _(chunk):
+            exchange(chunk)
+
+    def consume(start, count, last):
+        @pl.loop(start // CHUNK, (start + count) // CHUNK)
         def _(chunk):
             arrived(source, source_sem, chunk)
 
-        piece = pl.ds(index * TILE, TILE)
+        piece = pl.ds(start, count)
         part[piece] = jnp.dot(
             source[piece], right_zero[...], preferred_element_type=jnp.float32
         ).astype(jnp.bfloat16)
@@ -309,21 +318,28 @@
 
     told(1)
     tell(2)
-    consume(0, False)
-
-    @pl.loop(16, 24)
+    envs[2].wait()
+    envs[3].wait()
+    consume(0, 256, False)
+
+    @pl.loop(CHUNKS // 2, 3 * CHUNKS // 4)
     def _(chunk):
         exchange(chunk)
 
-    consume(1, False)
-
-    @pl.loop(24, 32)
+    consume(256, 256, False)
+
+    @pl.loop(3 * CHUNKS // 4, CHUNKS)
     def _(chunk):
         exchange(chunk)
 
     told(2)
-    consume(2, False)
-    consume(3, True)
+    peers = [
+        [place(phase_peer(k, phase, step)) for step in phase_steps(phase)]
+        for phase in range(len(PHASES))
+    ]
+    consume(512, 256, False)
+    consume(768, 128, False)
+    consume(896, 128, True)
 
     for phase, (stride, size) in enumerate(PHASES):
         digit = lax.rem(lax.div(k, stride), size)
@@ -332,13 +348,13 @@
         else:
             total = jnp.sum(slots[phase - 1, 0 : PHASES[phase - 1][1]], axis=0)
         slots[phase, digit] = total
-        for step in phase_steps(phase):
+        for peer in peers[phase]:
             pltpu.make_async_remote_copy(
                 src_ref=slots.at[phase, digit],
                 dst_ref=slots.at[phase, digit],
                 send_sem=sum_send.at[phase],
                 recv_sem=sum_recv.at[phase],
-                device_id=place(phase_peer(k, phase, step)),
+                device_id=peer,
                 device_id_type=MESH,
             ).start()
         others = slots.at[phase, pl.ds(0, size - 1)]
@@ -368,29 +384,45 @@
     @pl.when(is_low)
     def _():
         sent(0, CHUNKS)
-        sent(1, CHUNKS - MERGED_UP)
-        sent(2, MERGED_UP)
-        sent(3, CHUNKS - MERGED_UP)
 
     @pl.when(is_high)
     def _():
-        sent(1, MERGED_UP)
         sent(2, CHUNKS)
-        sent(3, CHUNKS - MERGED_UP)
-
-
-def finish_kernel(sums, image, masked, next_vector, coefficients, result, sem):
+
+    for i in range(4):
+        up = MERGED_UP[i]
+
+        @pl.when(is_low & (target_z(target) == i))
+        def _():
+            sent(1, CHUNKS - up)
+            sent(2, up)
+
+        @pl.when(is_low & (target_z(onward) == i))
+        def _():
+            sent(3, CHUNKS - up)
+
+        @pl.when(is_high & (target_z(target) == i))
+        def _():
+            sent(1, up)
+            sent(3, CHUNKS - up)
+
+
+def finish_kernel(sums, image, masked, next_vector, coefficients, result, pair, sem, pair_sem):
     slope = sums[0, 0:1, 0:1]
     gain = sums[1, 0:1, 0:1]
     copies = []
-    for i in range(LOADS):
-        at = pl.ds(i * LOAD, LOAD)
+    for i in range(SEC // OUT):
+        at = pl.ds(i * OUT, OUT)
         result[at] = (image[at] - slope * masked[at]) * gain
         copy = pltpu.make_async_copy(result.at[at], next_vector.at[0, at], sem.at[i])
         copy.start()
         copies.append(copy)
-    coefficients[0] = jnp.max(sums[0])
-    coefficients[1] = jnp.max(sums[2])
+        if i == 0:
+            pair[0] = jnp.max(sums[0])
+            pair[1] = jnp.max(sums[2])
+            copy = pltpu.make_async_copy(pair, coefficients, pair_sem)
+            copy.start()
+            copies.append(copy)
     for copy in copies:
         copy.wait()
 
@@ -437,8 +469,11 @@
             jax.ShapeDtypeStruct((2,), jnp.float32),
         ),
         in_specs=[vmem, vmem, vmem],
-        out_specs=(hbm, smem),
-        scratch_shapes=[pltpu.VMEM((SEC, SEC), jnp.float32), dma((LOADS,))],
+        out_specs=(hbm, hbm),
+        scratch_shapes=[
+            pltpu.VMEM((SEC, SEC), jnp.float32), pltpu.SMEM((2,), jnp.float32),
+            dma((SEC // OUT,)), dma,
+        ],
         compiler_params=pltpu.CompilerParams(vmem_limit_bytes=16 * 1024 * 1024),
         cost_estimate=pl.CostEstimate(flops=3 * SEC**2, bytes_accessed=4 << 20, transcendentals=0),
     )(sums, image, masked)

time: 69.1 us -> 67.3 us (0.974)
  the two profiles are of different devices: /device:TPU:1 before, /device:TPU:34 now
where the time goes in v3:
time: 67.3 us; the launch traced here: 67.2 us
  Pallas kernels  66.5 us (99%)
    pallas_call x1, Pallas kernels, per_device(): pl.pallas_call(step_kernel, out_shape=(jax.ShapeDtypeStruct((SEC, SEC), j...  64.3 us
    pallas_call x1, Pallas kernels, per_device(): pl.pallas_call(finish_kernel, out_shape=(jax.ShapeDtypeStruct((1, SEC, SE...  2.23 us

profile of v3, /device:TPU:34, one launch (start us, length us, event | category | flops | bytes accessed | tf_op | source)
XLA Modules:
  0.0 67.2 jit_solution(259999510757990623)
XLA Ops:
  0.6 64.3 %shard_map.77 = (f32[1024,1024]{1,0:T(8,128)S(1)}, f32[1024,1024]{1,0:T(8,128)S(1)}, f32[3,8,128]{2,1,0:T(8,128)S(1)}) custom-call(f32[2,4,4]{2,1,0:T(4,128)} %site_hbm.1, s32[32]{0:T(128)} %left_hbm.1, s32[34]{0:T(128)} %right_hbm.1, f32[1,1024,1024]{2,1,0:T(8,128)} %state.1, bf16[2,1,1024,1024]{3,2,1,0:T(8,128)(2,1)} %left_env.1, ...), custom_call_target="tpu_custom_call" | custom-call | flops 8589934592 | bytes 20971520 | tf_op jit(solution)/shard_map/pallas_call | solution.py:440
  64.9 2.2 %shard_map.78 = (f32[1,1024,1024]{2,1,0:T(8,128)}, f32[2]{0:T(128)}) custom-call(f32[3,8,128]{2,1,0:T(8,128)S(1)} %get-tuple-element.5.sums, f32[1024,1024]{1,0:T(8,128)S(1)} %get-tuple-element.6.image, f32[1024,1024]{1,0:T(8,128)S(1)} %get-tuple-element.7.masked), custom_call_target="tpu_custom_call" | custom-call | flops 3145728 | bytes 4194304 | tf_op jit(solution)/shard_map/pallas_call | solution.py:465

commit v4 on v3

--- a/solution.py
+++ b/solution.py
@@ -12,12 +12,13 @@
 DEVICES = 128
 CHUNK = 32
 CHUNKS = SEC // CHUNK
-MERGED_UP = (13, 13, 15, 15)
+MERGED_UP = (15, 14, 15, 15)
 LOAD = 128
 LOADS = SEC // LOAD
 OUT = 64
 TILE = 256
 TILES = SEC // TILE
+LAG = 3
 PHASES = ((1, 8), (8, 16))
 ROUNDS = 3
 
@@ -228,6 +229,12 @@
         at = tile_at(index)
         image[at] = diagonal * jnp.dot(left_one[at], part[...], preferred_element_type=jnp.float32)
 
+    def pass_on(chunk):
+        @pl.when(jnp.logical_not(goes_up(chunk, onward)))
+        def _():
+            arrived(first, first_sem, chunk)
+            send(first, source, 3, source_sem, chunk, onward)
+
     def exchange(chunk):
         up = goes_up(chunk, target)
 
@@ -257,10 +264,9 @@
             def _():
                 send(second, first, 3, first_sem, chunk, relay)
 
-        @pl.when(is_low & jnp.logical_not(goes_up(chunk, onward)))
-        def _():
-            arrived(first, first_sem, chunk)
-            send(first, source, 3, source_sem, chunk, onward)
+        @pl.when((chunk >= LAG) & is_low)
+        def _():
+            pass_on(jnp.maximum(chunk - LAG, 0))
 
     def tell(round_sem):
         for block in near:
@@ -320,17 +326,27 @@
     tell(2)
     envs[2].wait()
     envs[3].wait()
-    consume(0, 256, False)
-
-    @pl.loop(CHUNKS // 2, 3 * CHUNKS // 4)
+    @pl.loop(16, 20)
     def _(chunk):
         exchange(chunk)
 
-    consume(256, 256, False)
-
-    @pl.loop(3 * CHUNKS // 4, CHUNKS)
+    consume(0, 256, False)
+
+    @pl.loop(20, 28)
     def _(chunk):
         exchange(chunk)
+
+    consume(256, 256, False)
+
+    @pl.loop(28, 32)
+    def _(chunk):
+        exchange(chunk)
+
+    @pl.when(is_low)
+    def _():
+        @pl.loop(CHUNKS - LAG, CHUNKS)
+        def _(chunk):
+            pass_on(chunk)
 
     told(2)
     peers = [

time: 67.3 us -> 66.1 us (0.982)
  the two profiles are of different devices: /device:TPU:34 before, /device:TPU:1 now
where the time goes in v4:
time: 66.1 us; the launch traced here: 66 us
  Pallas kernels  65.3 us (99%)
    pallas_call x1, Pallas kernels, per_device(): pl.pallas_call(step_kernel, out_shape=(jax.ShapeDtypeStruct((SEC, SEC), j...  63.1 us
    pallas_call x1, Pallas kernels, per_device(): pl.pallas_call(finish_kernel, out_shape=(jax.ShapeDtypeStruct((1, SEC, SE...  2.23 us

profile of v4, /device:TPU:1, one launch (start us, length us, event | category | flops | bytes accessed | tf_op | source)
XLA Modules:
  0.0 66.0 jit_solution(11970269168298207935)
XLA Ops:
  0.6 63.1 %shard_map.77 = (f32[1024,1024]{1,0:T(8,128)S(1)}, f32[1024,1024]{1,0:T(8,128)S(1)}, f32[3,8,128]{2,1,0:T(8,128)S(1)}) custom-call(f32[2,4,4]{2,1,0:T(4,128)} %site_hbm.1, s32[32]{0:T(128)} %left_hbm.1, s32[34]{0:T(128)} %right_hbm.1, f32[1,1024,1024]{2,1,0:T(8,128)} %state.1, bf16[2,1,1024,1024]{3,2,1,0:T(8,128)(2,1)} %left_env.1, ...), custom_call_target="tpu_custom_call" | custom-call | flops 8589934592 | bytes 20971520 | tf_op jit(solution)/shard_map/pallas_call | solution.py:456
  63.8 2.2 %shard_map.78 = (f32[1,1024,1024]{2,1,0:T(8,128)}, f32[2]{0:T(128)}) custom-call(f32[3,8,128]{2,1,0:T(8,128)S(1)} %get-tuple-element.5.sums, f32[1024,1024]{1,0:T(8,128)S(1)} %get-tuple-element.6.image, f32[1024,1024]{1,0:T(8,128)S(1)} %get-tuple-element.7.masked), custom_call_target="tpu_custom_call" | custom-call | flops 3145728 | bytes 4194304 | tf_op jit(solution)/shard_map/pallas_call | solution.py:481
